TPU v7x, 128 devices: a whole 4x4x4 slice. The times are simulated.
128 devices in a mesh: tile: 8 (over y_lo, z), sub: 16 (over y_hi, x, core).
Axes of the slice: x: 4, y: 4 (y_hi: 2, y_lo: 2; y = y_hi * 2 + y_lo), z: 4, core: 2. Of those that a mesh axis runs over, the one named last changes fastest.
Arguments:
- initial: float32 [64, 128, 4096], P(None, 'tile', 'sub'), may hold values from -6 to 6
- targets: float32 [64, 128, 4096], P(None, 'tile', 'sub'), may hold values from -6 to 6
- diffusivity: float32 [128, 4096], P('tile', 'sub'), may hold values from 0.02 to 0.24
- column_order: int32 [128, 4096], P(('tile', 'sub')), may hold values from 0 to 4095, each once within a row
- send_counts: int32 [128, 128], P(('tile', 'sub')), may hold values from 0 to 64, as said below
- w_first: bfloat16 [16, 64, 192], P('sub'), may hold values from -0.75 to 0.75
- w_inner: bfloat16 [16, 3, 192, 192], P('sub'), may hold values from -0.4375 to 0.4375
- w_last: bfloat16 [16, 192, 64], P('sub'), may hold values from -0.4375 to 0.4375
- b_inner: float32 [16, 4, 192], P('sub'), may hold values from -2 to 2
- b_last: float32 [16, 64], P('sub'), may hold values from -2 to 2
Outputs:
- grad_initial: float32 [64, 128, 4096], P(None, 'tile', 'sub')
- step_first: float32 [16, 64, 192], P('sub')
- step_inner: float32 [16, 3, 192, 192], P('sub')
- step_last: float32 [16, 192, 64], P('sub')
- step_bias_inner: float32 [16, 4, 192], P('sub')
- step_bias_last: float32 [16, 64], P('sub')
Inputs may be any that keep to these rules, and one draw needn't show every extreme that they name: `send_counts`: each row sums to 4096. For every pair of destinations d and d plus half of 128 (same sub index, tile indices half the tile axis apart) the two entries of a row sum to 64; some destination receives 64 from every device.
All inputs are finite; a program needn't handle non-finite values.
Results may differ from a plain program's by a relative error of at most 0.0095.
Values may be sent and summed in bfloat16 or wider, within the bound.
A program may use at most 64 MiB of HBM per device.

v0:
```python
import jax
import jax.numpy as jnp
from jax import lax
from jax.experimental import pallas as pl
from jax.experimental.pallas import tpu as pltpu
from jax.sharding import PartitionSpec as P

MESH = pl.DeviceIdType.MESH
F32 = jnp.float32
BF16 = jnp.bfloat16
LEV = 64
WIDTH = 192
CX = 16
CY = 256
NCOL = CX * CY
TILES = 8
SUBS = 16
SHARE = NCOL // SUBS
PARAMS = 136000
AUG = 16
LANES = 128
SPAN = CY + LANES
SLABS = CX + 4
CHUNK = 96
GRAD_ROWS = CHUNK * TILES
FIRST_INNER = LEV + AUG
FIRST_LAST = FIRST_INNER + 3 * (WIDTH + AUG)
ANY = pl.BlockSpec(memory_space=pl.ANY)
LIMIT = 58 * 2**20


def wrapped(index, step, count):
    return lax.rem(index + step + count, count)


def remote(source, target, send_sem, recv_sem, peer):
    return pltpu.make_async_remote_copy(
        src_ref=source,
        dst_ref=target,
        send_sem=send_sem,
        recv_sem=recv_sem,
        device_id=peer,
        device_id_type=MESH,
    )


def tiled(block):
    return block.reshape(LEV, CX // 8, 8, 2, LANES).transpose(0, 1, 3, 2, 4).reshape(-1, LANES)


def untiled(rows):
    return rows.reshape(LEV, CX // 8, 2, 8, LANES).transpose(0, 1, 3, 2, 4).reshape(LEV, CX, CY)


def tiled_row(x, half):
    return (x // 8) * 16 + half * 8 + x % 8


def lanes(shape):
    return lax.broadcasted_iota(jnp.int32, shape, 1)


def sublanes(shape):
    return lax.broadcasted_iota(jnp.int32, shape, 0)


def dot(left, right, contract=(1, 0)):
    return lax.dot_general(
        left, right, (((contract[0],), (contract[1],)), ((), ())), preferred_element_type=F32
    )


def near_sum(value):
    return pltpu.roll(value, 1, 1) + pltpu.roll(value, SPAN - 1, 1)


def silu_and_slope(preact):
    sigmoid_value = 0.5 + 0.5 * jnp.tanh(0.5 * preact)
    active = preact * sigmoid_value
    return active.astype(BF16), sigmoid_value + active * (1.0 - sigmoid_value)


def find_routes(order, counts, sub, routes, tables, sems):
    count_row = counts[...]
    square = (TILES * SUBS, TILES * SUBS)
    earlier = lanes(square)

    def starts_and_shift(device):
        before = earlier < device
        same = earlier % SUBS == device % SUBS
        start = jnp.sum(jnp.where(before, count_row, 0), axis=1, keepdims=True)
        within = jnp.sum(jnp.where(before & same, count_row, 0), axis=1, keepdims=True)
        block = lax.rem(device[:, 0:1] % SUBS - sub + SUBS, SUBS)
        return start, block * SHARE + within - start

    device = sublanes(square)
    start, shift = starts_and_shift(device)
    _, shift_before = starts_and_shift(jnp.maximum(device - 1, 0))
    change = shift - jnp.where(device[:, 0:1] == 0, 0, shift_before)
    width = 512
    outward = jnp.zeros((32, 256), F32)
    homeward = jnp.zeros((32, 256), F32)

    def spread(where, what):
        high = (sublanes((32, width)) == where // LANES).astype(F32).astype(BF16)
        hit = sublanes((LANES, width)) == where % LANES
        values = jnp.concatenate(
            [jnp.where(hit, what // LANES, 0), jnp.where(hit, what % LANES, 0)], axis=0
        )
        return dot(high, values.astype(F32).astype(BF16), (1, 1))

    for first in range(0, NCOL, width):
        place = lanes((1, width)) + first
        slot = place + jnp.sum(jnp.where(start <= place, change, 0), axis=0, keepdims=True)
        column = order[:, first : first + width]
        outward = outward + spread(slot, column)
        homeward = homeward + spread(column, slot)
    for k, table in enumerate((outward, homeward)):
        whole = table.astype(jnp.int32)
        tables[k] = jnp.clip(whole[:, 0:LANES] * LANES + whole[:, LANES:], 0, NCOL - 1)
    for k in range(2):
        copy = pltpu.make_async_copy(tables.at[k], routes.at[k], sems.at[k])
        copy.start()
        copy.wait()


def step_kernel(
    initial_hbm, targets_hbm, diffusivity_hbm, order_hbm, counts_hbm,
    w_first_hbm, w_inner_hbm, w_last_hbm, b_inner_hbm, b_last_hbm,
    result_hbm, step_first_hbm, step_inner_hbm, step_last_hbm, step_bias_inner_hbm, step_bias_last_hbm,
    initial, targets, diffusivity, order, counts, w_first, w_inner, w_last_t, b_inner, b_last,
    result, step_first, step_inner, step_last_t, step_bias_inner, step_bias_last,
    load_sem, store_sem,
    field, middle, rates, columns, tables, routes,
    xs, xr, ys, yr, cs, cr, gxs, gxr, gys, gyr, gcs, gcr,
    wt_first, wt_inner, w_last, bias,
    stage, send, recv, answer, back, rows, grads, total, wide, parts, whole,
    table_sem, halo_sem, halo_in_sem, ghalo_sem, ghalo_in_sem,
    out_sem, in_sem, ret_sem, back_sem, part_sem, part_in_sem, whole_sem, whole_in_sem,
):
    tile, sub = lax.axis_index("tile"), lax.axis_index("sub")
    up, down = wrapped(tile, 1, TILES), wrapped(tile, -1, TILES)
    right, left = wrapped(sub, 1, SUBS), wrapped(sub, -1, SUBS)
    around = (
        (down, sub), (up, sub), (tile, left), (tile, right),
        (down, left), (down, right), (up, left), (up, right),
    )
    peers = (
        [(tile, wrapped(sub, j, SUBS)) for j in range(1, SUBS)]
        + [(wrapped(tile, j, TILES), sub) for j in range(1, TILES)]
        + list(around[4:])
    )
    barrier = pltpu.get_barrier_semaphore()
    for peer in peers:
        pl.semaphore_signal(barrier, inc=1, device_id=peer, device_id_type=MESH)

    loads = [
        pltpu.make_async_copy(source, target, load_sem.at[k])
        for k, (source, target) in enumerate(
            (
                (initial_hbm, initial), (diffusivity_hbm, diffusivity), (order_hbm, order),
                (counts_hbm, counts), (w_first_hbm, w_first), (w_inner_hbm, w_inner),
                (w_last_hbm, w_last_t), (b_inner_hbm, b_inner), (b_last_hbm, b_last),
                (targets_hbm, targets),
            )
        )
    ]
    for load in loads:
        load.start()
    stores = [
        pltpu.make_async_copy(source, target, store_sem.at[k])
        for k, (source, target) in enumerate(
            (
                (result, result_hbm), (step_first, step_first_hbm), (step_inner, step_inner_hbm),
                (step_last_t, step_last_hbm), (step_bias_inner, step_bias_inner_hbm),
                (step_bias_last, step_bias_last_hbm),
            )
        )
    ]

    def cells(ref, x):
        return jnp.concatenate(
            [ref[pl.ds(tiled_row(x, h), LEV, stride=2 * CX), :] for h in range(2)], axis=1
        )

    def halo(group, k, sends, receives, out_sems, in_sems):
        place = {"x": k, "y": 2 + k, "c": 4 + k}[group]
        other = (3 - k) if group == "c" else (1 - k)
        opposite = place - k + other
        return remote(
            sends.at[k], receives.at[other], out_sems.at[place], in_sems.at[opposite], around[place]
        )

    def strip(tile_of, side):
        pair = lanes((LEV, LANES)) // 2
        packed = jnp.zeros((LEV, LANES), F32)
        for x in range(CX):
            moved = tile_of(x, side)
            shift = (2 * x + 2 * side) % LANES
            if shift:
                moved = pltpu.roll(moved, shift, 1)
            packed = jnp.where(pair == x, moved, packed)
        return packed

    def edge_tile(x, side):
        return field[x + 2, :, side * LANES : (side + 1) * LANES]

    low = lanes((LEV, LANES)) < LEV

    def halo_tile(from_left, from_right, x):
        back_right = pltpu.roll(from_right, LANES - 2 * x, 1) if x else from_right
        return jnp.where(low, back_right, pltpu.roll(from_left, LANES - 2 - 2 * x, 1))

    def fill(x, carry):
        field[x + 2, :, 0:CY] = cells(initial, x)
        return carry

    loads[0].wait()
    loads[1].wait()
    lax.fori_loop(0, CX, fill, 0)
    for side in range(2):
        for k in range(2):
            xs[side, k * LEV : (k + 1) * LEV, :] = field[2 + (k if side == 0 else CX - 2 + k), :, 0:CY]
        xs[side, 2 * LEV :, :] = diffusivity[8 * side : 8 * side + 8, :]
    for corner in range(4):
        side, edge = corner // 2, corner % 2
        cs[corner, 0:LEV, :] = edge_tile(0 if side == 0 else CX - 1, edge)
        cs[corner, LEV:, :] = diffusivity[8 * side : 8 * side + 8, edge * LANES : (edge + 1) * LANES]
    pl.semaphore_wait(barrier, len(peers))
    copies = []
    for side in range(2):
        copies.append(halo("x", side, xs, xr, halo_sem, halo_in_sem))
        copies[-1].start()
    for corner in range(4):
        copies.append(halo("c", corner, cs, cr, halo_sem, halo_in_sem))
        copies[-1].start()
    for side in range(2):
        ys[side, 0:LEV, :] = strip(edge_tile, side)
        ys[side, LEV:, :] = diffusivity[:, side * LANES : (side + 1) * LANES]
        copies.append(halo("y", side, ys, yr, halo_sem, halo_in_sem))
        copies[-1].start()

    for load in loads[2:]:
        load.wait()
    find_routes(order, counts, sub, routes, tables, table_sem)
    same = sublanes((WIDTH, WIDTH)) == lanes((WIDTH, WIDTH))
    unit = same.astype(F32).astype(BF16)
    wt_first[...] = dot(unit, w_first[...], (1, 1)).astype(BF16)
    for k in range(3):
        wt_inner[k] = dot(unit, w_inner[k], (1, 1)).astype(BF16)
    w_last[...] = dot(unit, w_last_t[...], (1, 1)).astype(BF16)
    for k in range(4):
        bias[k] = jnp.sum(jnp.where(same, b_inner[k : k + 1, :], 0.0), axis=1, keepdims=True)
    same_lev = sublanes((LEV, LEV)) == lanes((LEV, LEV))
    bias[4, 0:LEV, :] = jnp.sum(jnp.where(same_lev, b_last[...], 0.0), axis=1, keepdims=True)
    total[...] = jnp.zeros_like(total)

    for copy in copies:
        copy.wait_recv()
    rates[0:2, 0:CY] = xr[0, 2 * LEV + 6 :, :]
    rates[2 : CX + 2, 0:CY] = diffusivity[...]
    rates[CX + 2 : CX + 4, 0:CY] = xr[1, 2 * LEV : 2 * LEV + 2, :]
    first_rows = lanes((CX, LANES)) < LEV
    rates[0:8, CY:] = jnp.zeros((8, LANES), F32)
    rates[16:24, CY:] = jnp.zeros((8, LANES), F32)
    rates[2 : CX + 2, CY:] = jnp.where(first_rows, yr[1, LEV:, :], yr[0, LEV:, :])
    one_row = lanes((1, LANES)) < LEV
    rates[1:2, CY:] = jnp.where(one_row, cr[1, LEV + 7 :, :], cr[0, LEV + 7 :, :])
    rates[CX + 2 : CX + 3, CY:] = jnp.where(
        one_row, cr[3, LEV : LEV + 1, :], cr[2, LEV : LEV + 1, :]
    )

    def spread_halo(x_in, y_in, c_in):
        for side in range(2):
            for k in range(2):
                slab = k if side == 0 else CX + 2 + k
                field[slab, :, 0:CY] = x_in[side, k * LEV : (k + 1) * LEV, :].astype(F32)
            outer = 0 if side == 0 else CX + 3
            field[outer, :, CY:] = jnp.zeros((LEV, LANES), F32)
            inner = 1 if side == 0 else CX + 2
            field[inner, :, CY:] = jnp.where(
                low, c_in[2 * side + 1, 0:LEV, :].astype(F32), c_in[2 * side, 0:LEV, :].astype(F32)
            )
        from_left, from_right = y_in[0, 0:LEV, :].astype(F32), y_in[1, 0:LEV, :].astype(F32)
        for x in range(CX):
            field[x + 2, :, CY:] = halo_tile(from_left, from_right, x)

    spread_halo(xr, yr, cr)

    def diffused(ref, slab):
        now = ref[slab]
        near = ref[slab - 1] + ref[slab + 1] + near_sum(now)
        return now + rates[pl.ds(slab, 1), :] * (near - 4.0 * now)

    def forward_first(slab, carry):
        middle[slab] = diffused(field, slab)
        return carry

    lax.fori_loop(1, CX + 3, forward_first, 0)

    def forward_second(x, carry):
        later = diffused(middle, x + 2)[:, 0:CY]
        both = jnp.concatenate([later, later - cells(targets, x)], axis=0)
        columns[pl.ds(pl.multiple_of(x * CY, CY), CY), :] = both.T
        return carry

    lax.fori_loop(0, CX, forward_second, 0)

    def outgoing(j):
        return remote(send.at[j], recv.at[j], out_sem.at[j], in_sem.at[j], (tile, wrapped(sub, j, SUBS)))

    def returning(j):
        return remote(answer.at[j], back.at[j], ret_sem.at[j], back_sem.at[j], (tile, wrapped(sub, -j, SUBS)))

    def gathered(j):
        def some(group, carry):
            base = group * 16
            line = j * 2 + group // 8
            taken = [columns[pl.ds(routes[0, line, (group % 8) * 16 + k], 1), :] for k in range(16)]
            for k in range(16):
                stage[pl.ds(base + k, 1), :] = taken[k]
            return carry

        lax.fori_loop(0, SHARE // 16, some, 0)
        return stage[...].astype(BF16)

    def push(j, carry):
        send[j] = gathered(j)
        outgoing(j).start()
        return carry

    lax.fori_loop(1, SUBS, push, 0)
    recv[0] = gathered(0)

    extra = (sublanes((AUG, SHARE)) == 0).astype(F32).astype(BF16)

    def with_ones(value):
        return jnp.concatenate([value, extra], axis=0)

    def two_blocks(pair, carry):
        @pl.when(pair > 0)
        def _():
            outgoing(2 * pair).wait_recv()

        outgoing(2 * pair + 1).wait_recv()
        both = range(2)
        turned = [recv[2 * pair + b].astype(F32).T for b in both]
        inputs = [turned[b][:LEV].astype(BF16) for b in both]
        current = inputs
        feeds, slopes = [inputs], []
        for k in range(4):
            weight = wt_first[...] if k == 0 else wt_inner[k - 1]
            outs = [silu_and_slope(dot(weight, current[b]) + bias[k]) for b in both]
            current = [outs[b][0] for b in both]
            feeds.append(current)
            slopes.append([outs[b][1] for b in both])
        residue = [
            turned[b][LEV:] + dot(w_last_t[...], current[b]) + bias[4, 0:LEV, :] for b in both
        ]
        error = [residue[b].astype(BF16) for b in both]
        total[FIRST_LAST:, 0 : WIDTH + AUG] += sum(
            dot(error[b], with_ones(current[b]), (1, 1)) for b in both
        )
        carried = [dot(w_last[...], error[b]) for b in both]
        for k in (3, 2, 1, 0):
            error = [(carried[b] * slopes[k][b]).astype(BF16) for b in both]
            row = FIRST_INNER + (k - 1) * (WIDTH + AUG) if k else 0
            high = (WIDTH if k else LEV) + AUG
            total[row : row + high, 0:WIDTH] += sum(
                dot(with_ones(feeds[k][b]), error[b], (1, 1)) for b in both
            )
            weight = w_inner[k - 1] if k else w_first[...]
            carried = [dot(weight, error[b]) for b in both]
        half = SHARE // 2
        for b in both:
            outcome = residue[b] + carried[b]
            packed = jnp.concatenate([outcome[:, :half], outcome[:, half:]], axis=0)
            answer[2 * pair + b] = packed.T.astype(BF16)

        @pl.when(pair > 0)
        def _():
            returning(2 * pair).start()

        returning(2 * pair + 1).start()
        return carry

    lax.fori_loop(0, SUBS // 2, two_blocks, 0)

    wide[...] = total[...].astype(BF16)

    def part(j):
        owner = wrapped(tile, j, TILES)
        first = pl.multiple_of(owner * CHUNK, CHUNK)
        return remote(
            wide.at[pl.ds(first, CHUNK)], parts.at[j], part_sem.at[j], part_in_sem.at[j], (owner, sub)
        )

    def share_of(j):
        return remote(
            whole.at[0], whole.at[j], whole_sem.at[j], whole_in_sem.at[j], (wrapped(tile, j, TILES), sub)
        )

    for j in range(1, TILES):
        part(j).start()

    def unpack(j, source):
        block = source.astype(F32)
        first = pl.multiple_of(j * SHARE, SHARE)
        rows[pl.ds(first, SHARE // 2), :] = block
        rows[pl.ds(first + SHARE // 2, SHARE // 2), :] = pltpu.roll(block, LEV, 1)

    unpack(0, answer[0])

    def take(j, carry):
        returning(j).wait_recv()
        unpack(j, back[j])
        return carry

    lax.fori_loop(1, SUBS, take, 0)

    left_half = lanes((CY, LANES)) < LEV

    def home(x):
        def some(group, carry):
            base = group * 16
            line = x * 2 + group // 8
            taken = [rows[pl.ds(routes[1, line, (group % 8) * 16 + k], 1), :] for k in range(16)]
            for k in range(16):
                grads[pl.ds(base + k, 1), :] = taken[k]
            return carry

        lax.fori_loop(0, 2 * CY // 16, some, 0)
        turned = jnp.where(left_half, grads[0:CY, :], pltpu.roll(grads[CY:, :], LEV, 1)).T
        for k in range(2):
            field[x + k + 2, :, 0:CY] = turned[k * LEV : (k + 1) * LEV]

    copies = list(copies)
    ghalos = []
    for side in range(2):
        x = 0 if side == 0 else CX - 2
        home(x)
        for k in range(2):
            gxs[side, k * LEV : (k + 1) * LEV, :] = field[x + k + 2, :, 0:CY].astype(BF16)
        for edge in range(2):
            gcs[2 * side + edge] = edge_tile(0 if side == 0 else CX - 1, edge).astype(BF16)
        ghalos.append(halo("x", side, gxs, gxr, ghalo_sem, ghalo_in_sem))
        for edge in range(2):
            ghalos.append(halo("c", 2 * side + edge, gcs, gcr, ghalo_sem, ghalo_in_sem))
        for copy in ghalos[-3:]:
            copy.start()

    mine = pl.multiple_of(tile * CHUNK, CHUNK)
    summed = wide[pl.ds(mine, CHUNK), :].astype(F32)
    for j in range(1, TILES):
        part(j).wait_recv()
        summed = summed + parts[j].astype(F32)
    whole[0] = summed.astype(BF16)
    for j in range(1, TILES):
        share_of(j).start()

    def home_pair(pair, carry):
        home(2 * pair)
        return carry

    lax.fori_loop(1, CX // 2 - 1, home_pair, 0)
    for side in range(2):
        gys[side] = strip(edge_tile, side).astype(BF16)
        ghalos.append(halo("y", side, gys, gyr, ghalo_sem, ghalo_in_sem))
        ghalos[-1].start()

    for j in range(1, TILES):
        share_of(j).wait_recv()
    for j in range(TILES):
        owner = wrapped(tile, -j, TILES)
        total[pl.ds(pl.multiple_of(owner * CHUNK, CHUNK), CHUNK), :] = whole[j].astype(F32)
    everything = total[...]
    squares = jnp.sum(jnp.sum(everything * everything, axis=0, keepdims=True), axis=1, keepdims=True)
    factor = lax.rsqrt(squares / PARAMS + 1e-06)
    step_first[...] = total[0:LEV, 0:WIDTH] * factor
    step_bias_inner[0:1, :] = total[LEV : LEV + 1, 0:WIDTH] * factor
    for k in range(3):
        row = FIRST_INNER + k * (WIDTH + AUG)
        step_inner[k] = total[row : row + WIDTH, 0:WIDTH] * factor
        step_bias_inner[k + 1 : k + 2, :] = total[row + WIDTH : row + WIDTH + 1, 0:WIDTH] * factor
    step_last_t[...] = total[FIRST_LAST:, 0:WIDTH] * factor
    last_bias = total[FIRST_LAST:, WIDTH : WIDTH + 1] * factor
    step_bias_last[...] = jnp.sum(jnp.where(same_lev, last_bias, 0.0), axis=0, keepdims=True)
    for store in stores[1:]:
        store.start()

    for copy in ghalos:
        copy.wait_recv()
    spread_halo(gxr, gyr, gcr)

    def adjoint(ref, slab):
        rate = [rates[pl.ds(slab + k, 1), :] for k in (-1, 0, 1)]
        now = ref[slab]
        flow = rate[1] * now
        near = rate[0] * ref[slab - 1] + rate[2] * ref[slab + 1] + near_sum(flow)
        return now + (near - 4.0 * flow)

    def adjoint_first(slab, carry):
        middle[slab] = adjoint(field, slab)
        return carry

    lax.fori_loop(1, CX + 3, adjoint_first, 0)

    def adjoint_second(x, carry):
        done = adjoint(middle, x + 2)
        for h in range(2):
            result[pl.ds(tiled_row(x, h), LEV, stride=2 * CX), :] = done[:, h * LANES : (h + 1) * LANES]
        return carry

    lax.fori_loop(0, CX, adjoint_second, 0)

    stores[0].start()

    def settle(j, carry):
        outgoing(j).wait_send()
        returning(j).wait_send()
        return carry

    lax.fori_loop(1, SUBS, settle, 0)
    for j in range(1, TILES):
        part(j).wait_send()
        share_of(j).wait_send()
    for copy in copies + ghalos:
        copy.wait_send()
    for store in stores:
        store.wait()


def both_ways(shape, kind):
    return [pltpu.VMEM(shape, kind), pltpu.VMEM(shape, kind)]


def per_device(
    initial, targets, diffusivity, column_order, send_counts, w_first, w_inner, w_last, b_inner, b_last
):
    slabs = pltpu.VMEM((SLABS, LEV, SPAN), F32)
    result, step_first, step_inner, step_last_t, step_bias_inner, step_bias_last = pl.pallas_call(
        step_kernel,
        out_shape=(
            jax.ShapeDtypeStruct((LEV * CX * 2, LANES), F32),
            jax.ShapeDtypeStruct((LEV, WIDTH), F32),
            jax.ShapeDtypeStruct((3, WIDTH, WIDTH), F32),
            jax.ShapeDtypeStruct((LEV, WIDTH), F32),
            jax.ShapeDtypeStruct((4, WIDTH), F32),
            jax.ShapeDtypeStruct((1, LEV), F32),
        ),
        in_specs=[ANY] * 10,
        out_specs=(ANY,) * 6,
        scratch_shapes=[
            pltpu.VMEM((LEV * CX * 2, LANES), F32),
            pltpu.VMEM((LEV * CX * 2, LANES), F32),
            pltpu.VMEM((CX, CY), F32),
            pltpu.VMEM((1, NCOL), jnp.int32),
            pltpu.VMEM((1, TILES * SUBS), jnp.int32),
            pltpu.VMEM((LEV, WIDTH), BF16),
            pltpu.VMEM((3, WIDTH, WIDTH), BF16),
            pltpu.VMEM((LEV, WIDTH), BF16),
            pltpu.VMEM((4, WIDTH), F32),
            pltpu.VMEM((1, LEV), F32),
            pltpu.VMEM((LEV * CX * 2, LANES), F32),
            pltpu.VMEM((LEV, WIDTH), F32),
            pltpu.VMEM((3, WIDTH, WIDTH), F32),
            pltpu.VMEM((LEV, WIDTH), F32),
            pltpu.VMEM((4, WIDTH), F32),
            pltpu.VMEM((1, LEV), F32),
            pltpu.SemaphoreType.DMA((10,)),
            pltpu.SemaphoreType.DMA((6,)),
            slabs,
            slabs,
            pltpu.VMEM((24, SPAN), F32),
            pltpu.VMEM((NCOL, LANES), F32),
            pltpu.VMEM((2, NCOL // LANES, LANES), jnp.int32),
            pltpu.SMEM((2, NCOL // LANES, LANES), jnp.int32),
        ]
        + both_ways((2, 2 * LEV + 8, CY), F32)
        + both_ways((2, LEV + CX, LANES), F32)
        + both_ways((4, LEV + 8, LANES), F32)
        + both_ways((2, 2 * LEV, CY), BF16)
        + both_ways((2, LEV, LANES), BF16)
        + both_ways((4, LEV, LANES), BF16)
        + [
            pltpu.VMEM((WIDTH, LEV), BF16),
            pltpu.VMEM((3, WIDTH, WIDTH), BF16),
            pltpu.VMEM((WIDTH, LEV), BF16),
            pltpu.VMEM((5, WIDTH, 1), F32),
            pltpu.VMEM((SHARE, LANES), F32),
        ]
        + both_ways((SUBS, SHARE, LANES), BF16)
        + both_ways((SUBS, SHARE // 2, LANES), BF16)
        + [
            pltpu.VMEM((NCOL, LANES), F32),
            pltpu.VMEM((2 * CY, LANES), F32),
            pltpu.VMEM((GRAD_ROWS, 256), F32),
            pltpu.VMEM((GRAD_ROWS, 256), BF16),
        ]
        + both_ways((TILES, CHUNK, 256), BF16)
        + [pltpu.SemaphoreType.DMA((2,))]
        + [pltpu.SemaphoreType.DMA((8,))] * 4
        + [pltpu.SemaphoreType.DMA((SUBS,))] * 4
        + [pltpu.SemaphoreType.DMA((TILES,))] * 4,
        compiler_params=pltpu.CompilerParams(
            collective_id=0, has_side_effects=True, vmem_limit_bytes=LIMIT
        ),
        name="step",
    )(
        tiled(initial),
        tiled(targets),
        diffusivity,
        column_order,
        send_counts,
        w_first[0],
        w_inner[0],
        w_last[0].T,
        b_inner[0],
        b_last,
    )
    return (
        untiled(result),
        step_first[None],
        step_inner[None],
        step_last_t.T[None],
        step_bias_inner[None],
        step_bias_last,
    )


def solution(mesh):
    placed = (
        P(None, "tile", "sub"),
        P(None, "tile", "sub"),
        P("tile", "sub"),
        P(("tile", "sub"), None),
        P(("tile", "sub"), None),
        P("sub", None, None),
        P("sub", None, None, None),
        P("sub", None, None),
        P("sub", None, None),
        P("sub", None),
    )
    return jax.shard_map(
        per_device,
        mesh=mesh,
        in_specs=placed,
        out_specs=(
            P(None, "tile", "sub"),
            P("sub", None, None),
            P("sub", None, None, None),
            P("sub", None, None),
            P("sub", None, None),
            P("sub", None),
        ),
        check_vma=False,
    )
```

profile of v0, /device:TPU:7, one launch (start us, length us, event | category | flops | bytes accessed | tf_op | source)
XLA Modules:
  0.0 86.5 jit_solution(17092431770481493820)
XLA Ops:
  0.6 80.2 %step.1 = (f32[2048,128]{1,0:T(8,128)}, f32[64,192]{1,0:T(8,128)}, f32[3,192,192]{2,1,0:T(8,128)}, f32[64,192]{1,0:T(8,128)}, f32[4,192]{1,0:T(4,128)}, /*index=5*/f32[1,64]{1,0:T(1,128)}) custom-call(f32[2048,128]{1,0:T(8,128)} %bitcast.27, f32[2048,128]{1,0:T(8,128)} %bitcast.28, f32[16,256]{1,0:T(8,128)} %diffusivity_hbm.1, s32[1,4096]{1,0:T(1,128)} %order_hbm.1, ...), custom_call_target="tpu_custom_call" | custom-call | tf_op jit(solution)/shard_map/step/pallas_call | solution.py:541
  80.8 0.0 copy-start.2
  80.9 0.0 copy-start
  80.9 2.3 %copy.22 = f32[64,16,256]{2,1,0:T(8,128)} copy(f32[64,16,256]{2,1,0:T(8,128)} %bitcast.29) | data formatting | bytes 2097152
  83.2 0.0 copy-done.2
  83.2 0.6 copy.23
  83.8 0.0 copy-done
  83.8 0.0 copy-start.1
  83.8 0.8 copy.24
  84.6 0.0 copy-done.1
  84.7 0.0 copy-start.3
  84.7 0.6 copy.25
  85.3 0.0 copy-done.3
  85.4 0.0 copy-start.4
  85.4 0.6 copy.26
  86.0 0.1 copy-done.4
  86.0 0.5 copy.27
Async XLA Ops:
  80.8 2.4 %copy-start.2 = (f32[64,192]{1,0:T(8,128)S(1)}, f32[64,192]{1,0:T(8,128)}, u32[]{:S(2)}) copy-start(f32[64,192]{1,0:T(8,128)} %get-tuple-element.13) | copy-start | bytes 147460
  80.9 3.0 %copy-start = (f32[3,192,192]{2,1,0:T(8,128)S(1)}, f32[3,192,192]{2,1,0:T(8,128)}, u32[]{:S(2)}) copy-start(f32[3,192,192]{2,1,0:T(8,128)} %get-tuple-element.14) | copy-start | bytes 1327108
  83.8 0.9 copy-start.1
  84.7 0.7 copy-start.3
  85.4 0.7 copy-start.4
where the time goes:
time: 86.8 us; the launch traced here: 86.5 us
  Pallas kernels  80.2 us (92%)
  local copies, waits for them, and re-layouts  5.67 us (7%)
    pallas_call x1, Pallas kernels, per_device(): pl.pallas_call(step_kernel, out_shape=(jax.ShapeDtypeStruct((LEV * CX * 2...  80.2 us
    unnamed x16, local copies, waits for them, and re-layouts  5.67 us

commit v1 on v0

--- a/solution.py
+++ b/solution.py
@@ -22,6 +22,7 @@
 SPAN = CY + LANES
 SLABS = CX + 4
 CHUNK = 96
+GROUP = 4
 GRAD_ROWS = CHUNK * TILES
 FIRST_INNER = LEV + AUG
 FIRST_LAST = FIRST_INNER + 3 * (WIDTH + AUG)
@@ -312,39 +313,41 @@
     def returning(j):
         return remote(answer.at[j], back.at[j], ret_sem.at[j], back_sem.at[j], (tile, wrapped(sub, -j, SUBS)))
 
-    def gathered(j):
-        def some(group, carry):
-            base = group * 16
-            line = j * 2 + group // 8
-            taken = [columns[pl.ds(routes[0, line, (group % 8) * 16 + k], 1), :] for k in range(16)]
+    def gathered(table, line, source, target):
+        for first in range(0, LANES, 16):
+            taken = [source[pl.ds(routes[table, line, first + k], 1), :] for k in range(16)]
             for k in range(16):
-                stage[pl.ds(base + k, 1), :] = taken[k]
-            return carry
-
-        lax.fori_loop(0, SHARE // 16, some, 0)
-        return stage[...].astype(BF16)
-
-    def push(j, carry):
-        send[j] = gathered(j)
-        outgoing(j).start()
-        return carry
-
-    lax.fori_loop(1, SUBS, push, 0)
-    recv[0] = gathered(0)
+                target[first + k : first + k + 1, :] = taken[k]
+
+    def push(step, carry):
+        j = lax.rem(step, SUBS)
+        for half in range(2):
+            gathered(0, 2 * j + half, columns, stage.at[half])
+        send[j] = stage[...].reshape(SHARE, LANES).astype(BF16)
+
+        @pl.when(j > 0)
+        def _():
+            outgoing(j).start()
+
+        return carry
+
+    lax.fori_loop(1, SUBS + 1, push, 0)
+    recv[0] = send[0]
 
     extra = (sublanes((AUG, SHARE)) == 0).astype(F32).astype(BF16)
 
     def with_ones(value):
         return jnp.concatenate([value, extra], axis=0)
 
-    def two_blocks(pair, carry):
-        @pl.when(pair > 0)
+    def some_blocks(turn, carry):
+        @pl.when(turn > 0)
         def _():
-            outgoing(2 * pair).wait_recv()
-
-        outgoing(2 * pair + 1).wait_recv()
-        both = range(2)
-        turned = [recv[2 * pair + b].astype(F32).T for b in both]
+            outgoing(GROUP * turn).wait_recv()
+
+        for b in range(1, GROUP):
+            outgoing(GROUP * turn + b).wait_recv()
+        both = range(GROUP)
+        turned = [recv[GROUP * turn + b].astype(F32).T for b in both]
         inputs = [turned[b][:LEV].astype(BF16) for b in both]
         current = inputs
         feeds, slopes = [inputs], []
@@ -375,16 +378,17 @@
         for b in both:
             outcome = residue[b] + carried[b]
             packed = jnp.concatenate([outcome[:, :half], outcome[:, half:]], axis=0)
-            answer[2 * pair + b] = packed.T.astype(BF16)
-
-        @pl.when(pair > 0)
+            answer[GROUP * turn + b] = packed.T.astype(BF16)
+
+        @pl.when(turn > 0)
         def _():
-            returning(2 * pair).start()
-
-        returning(2 * pair + 1).start()
-        return carry
-
-    lax.fori_loop(0, SUBS // 2, two_blocks, 0)
+            returning(GROUP * turn).start()
+
+        for b in range(1, GROUP):
+            returning(GROUP * turn + b).start()
+        return carry
+
+    lax.fori_loop(0, SUBS // GROUP, some_blocks, 0)
 
     wide[...] = total[...].astype(BF16)
 
@@ -421,24 +425,26 @@
     left_half = lanes((CY, LANES)) < LEV
 
     def home(x):
-        def some(group, carry):
-            base = group * 16
-            line = x * 2 + group // 8
-            taken = [rows[pl.ds(routes[1, line, (group % 8) * 16 + k], 1), :] for k in range(16)]
-            for k in range(16):
-                grads[pl.ds(base + k, 1), :] = taken[k]
+        def some(line, carry):
+            gathered(1, x * 2 + line, rows, grads.at[line])
             return carry
 
-        lax.fori_loop(0, 2 * CY // 16, some, 0)
-        turned = jnp.where(left_half, grads[0:CY, :], pltpu.roll(grads[CY:, :], LEV, 1)).T
+        lax.fori_loop(0, 4, some, 0)
+        slab = [grads[2 * k : 2 * k + 2].reshape(CY, LANES) for k in range(2)]
+        turned = jnp.where(left_half, slab[0], pltpu.roll(slab[1], LEV, 1)).T
         for k in range(2):
             field[x + k + 2, :, 0:CY] = turned[k * LEV : (k + 1) * LEV]
 
     copies = list(copies)
     ghalos = []
+
+    def home_edge(side, carry):
+        home(side * (CX - 2))
+        return carry
+
+    lax.fori_loop(0, 2, home_edge, 0)
     for side in range(2):
         x = 0 if side == 0 else CX - 2
-        home(x)
         for k in range(2):
             gxs[side, k * LEV : (k + 1) * LEV, :] = field[x + k + 2, :, 0:CY].astype(BF16)
         for edge in range(2):
@@ -530,6 +536,20 @@
         store.wait()
 
 
+def copy_kernel(*refs):
+    sources, targets, held = refs[0:6], refs[6:12], refs[12:18]
+    in_sem, out_sem = refs[18:]
+    loads = [pltpu.make_async_copy(sources[k], held[k], in_sem.at[k]) for k in range(6)]
+    stores = [pltpu.make_async_copy(held[k], targets[k], out_sem.at[k]) for k in range(6)]
+    for load in loads:
+        load.start()
+    for load, store in zip(loads, stores):
+        load.wait()
+        store.start()
+    for store in stores:
+        store.wait()
+
+
 def both_ways(shape, kind):
     return [pltpu.VMEM(shape, kind), pltpu.VMEM(shape, kind)]
 
@@ -538,7 +558,7 @@
     initial, targets, diffusivity, column_order, send_counts, w_first, w_inner, w_last, b_inner, b_last
 ):
     slabs = pltpu.VMEM((SLABS, LEV, SPAN), F32)
-    result, step_first, step_inner, step_last_t, step_bias_inner, step_bias_last = pl.pallas_call(
+    made = pl.pallas_call(
         step_kernel,
         out_shape=(
             jax.ShapeDtypeStruct((LEV * CX * 2, LANES), F32),
@@ -587,13 +607,13 @@
             pltpu.VMEM((3, WIDTH, WIDTH), BF16),
             pltpu.VMEM((WIDTH, LEV), BF16),
             pltpu.VMEM((5, WIDTH, 1), F32),
-            pltpu.VMEM((SHARE, LANES), F32),
+            pltpu.VMEM((2, LANES, LANES), F32),
         ]
         + both_ways((SUBS, SHARE, LANES), BF16)
         + both_ways((SUBS, SHARE // 2, LANES), BF16)
         + [
             pltpu.VMEM((NCOL, LANES), F32),
-            pltpu.VMEM((2 * CY, LANES), F32),
+            pltpu.VMEM((4, LANES, LANES), F32),
             pltpu.VMEM((GRAD_ROWS, 256), F32),
             pltpu.VMEM((GRAD_ROWS, 256), BF16),
         ]
@@ -618,6 +638,15 @@
         b_inner[0],
         b_last,
     )
+    result, step_first, step_inner, step_last_t, step_bias_inner, step_bias_last = pl.pallas_call(
+        copy_kernel,
+        out_shape=tuple(jax.ShapeDtypeStruct(one.shape, one.dtype) for one in made),
+        in_specs=[ANY] * 6,
+        out_specs=(ANY,) * 6,
+        scratch_shapes=[pltpu.VMEM(one.shape, one.dtype) for one in made]
+        + [pltpu.SemaphoreType.DMA((6,))] * 2,
+        name="finish",
+    )(*made)
     return (
         untiled(result),
         step_first[None],

time: 86.8 us -> 70.7 us (0.81)
  the two profiles are of different devices: /device:TPU:7 before, /device:TPU:0 now
where the time goes in v1:
time: 70.7 us; the launch traced here: 69.6 us
  Pallas kernels  69 us (98%)
    pallas_call x1, Pallas kernels, per_device(): pl.pallas_call(step_kernel, out_shape=(jax.ShapeDtypeStruct((LEV * CX * 2...  66.5 us
    pallas_call x1, Pallas kernels, per_device(): pl.pallas_call(copy_kernel, out_shape=tuple((jax.ShapeDtypeStruct(one.sha...  2.52 us

profile of v1, /device:TPU:0, one launch (start us, length us, event | category | flops | bytes accessed | tf_op | source)
XLA Modules:
  0.0 69.6 jit_solution(15893166853181530195)
XLA Ops:
  0.6 66.5 %step.1 = (f32[2048,128]{1,0:T(8,128)}, f32[64,192]{1,0:T(8,128)}, f32[3,192,192]{2,1,0:T(8,128)}, f32[64,192]{1,0:T(8,128)}, f32[4,192]{1,0:T(4,128)}, /*index=5*/f32[1,64]{1,0:T(1,128)}) custom-call(f32[2048,128]{1,0:T(8,128)} %bitcast.27, f32[2048,128]{1,0:T(8,128)} %bitcast.28, f32[16,256]{1,0:T(8,128)} %diffusivity_hbm.1, s32[1,4096]{1,0:T(1,128)} %order_hbm.1, ...), custom_call_target="tpu_custom_call" | custom-call | tf_op jit(solution)/shard_map/step/pallas_call | solution.py:561
  67.1 2.5 %finish.1 = (f32[2048,128]{1,0:T(8,128)}, f32[64,192]{1,0:T(8,128)}, f32[3,192,192]{2,1,0:T(8,128)}, f32[64,192]{1,0:T(8,128)}, f32[4,192]{1,0:T(4,128)}, /*index=5*/f32[1,64]{1,0:T(1,128)}) custom-call(f32[2048,128]{1,0:T(8,128)} %get-tuple-element.18.refs_0_, f32[64,192]{1,0:T(8,128)} %get-tuple-element.19.refs_1_, ...), custom_call_target="tpu_custom_call" | custom-call | tf_op jit(solution)/shard_map/finish/pallas_call | solution.py:641

commit v2 on v1

--- a/solution.py
+++ b/solution.py
@@ -45,6 +45,26 @@
     )
 
 
+def gray(step):
+    return step + step // 2 - 2 * (step // 3)
+
+
+def partner(sub, j, sign):
+    late = jnp.minimum(j // 2, 1)
+    turned = late * (1 - j % 2) + (1 - late) * (j % 2)
+    x = gray(j // 2 % 4)
+    high = (sub // 8 + turned) % 2
+    middle = (sub // 2 + sign * x + 4) % 4
+    return high * 8 + middle * 2 + (sub + j // 8) % 2
+
+
+def place_of(sub, other):
+    turned = (other // 8 + sub // 8) % 2
+    step = (other + sub) % 2 * 4 + gray((other // 2 - sub // 2 + 8) % 4)
+    late = jnp.minimum(step, 1)
+    return 2 * step + late * (1 - turned) + (1 - late) * turned
+
+
 def tiled(block):
     return block.reshape(LEV, CX // 8, 8, 2, LANES).transpose(0, 1, 3, 2, 4).reshape(-1, LANES)
 
@@ -91,7 +111,7 @@
         same = earlier % SUBS == device % SUBS
         start = jnp.sum(jnp.where(before, count_row, 0), axis=1, keepdims=True)
         within = jnp.sum(jnp.where(before & same, count_row, 0), axis=1, keepdims=True)
-        block = lax.rem(device[:, 0:1] % SUBS - sub + SUBS, SUBS)
+        block = place_of(sub, device[:, 0:1] % SUBS)
         return start, block * SHARE + within - start
 
     device = sublanes(square)
@@ -135,7 +155,7 @@
     field, middle, rates, columns, tables, routes,
     xs, xr, ys, yr, cs, cr, gxs, gxr, gys, gyr, gcs, gcr,
     wt_first, wt_inner, w_last, bias,
-    stage, send, recv, answer, back, rows, grads, total, wide, parts, whole,
+    stage, send, recv, answer, back, rows, grads, edges, total, wide, parts, whole,
     table_sem, halo_sem, halo_in_sem, ghalo_sem, ghalo_in_sem,
     out_sem, in_sem, ret_sem, back_sem, part_sem, part_in_sem, whole_sem, whole_in_sem,
 ):
@@ -219,14 +239,22 @@
     loads[0].wait()
     loads[1].wait()
     lax.fori_loop(0, CX, fill, 0)
+    rate_high = diffusivity[...].astype(BF16)
+    rate_parts = (rate_high, (diffusivity[...] - rate_high.astype(F32)).astype(BF16))
+    same_lev = sublanes((LEV, LEV)) == lanes((LEV, LEV))
     for side in range(2):
         for k in range(2):
-            xs[side, k * LEV : (k + 1) * LEV, :] = field[2 + (k if side == 0 else CX - 2 + k), :, 0:CY]
-        xs[side, 2 * LEV :, :] = diffusivity[8 * side : 8 * side + 8, :]
+            edge = field[2 + (k if side == 0 else CX - 2 + k), :, 0:CY]
+            xs[side, k * LEV : (k + 1) * LEV, :] = edge.astype(BF16)
+        for k in range(2):
+            xs[side, 2 * LEV + k * CX : 2 * LEV + (k + 1) * CX, :] = rate_parts[k]
     for corner in range(4):
         side, edge = corner // 2, corner % 2
-        cs[corner, 0:LEV, :] = edge_tile(0 if side == 0 else CX - 1, edge)
-        cs[corner, LEV:, :] = diffusivity[8 * side : 8 * side + 8, edge * LANES : (edge + 1) * LANES]
+        x = 0 if side == 0 else CX - 1
+        y = edge * (CY - 1)
+        cell = jnp.where(same_lev, field[x + 2, :, y : y + 1], 0.0)
+        cs[corner, 0:1, 0:LEV] = jnp.sum(cell, axis=0, keepdims=True)
+        cs[corner, 1:2, :] = diffusivity[x : x + 1, edge * LANES : (edge + 1) * LANES]
     pl.semaphore_wait(barrier, len(peers))
     copies = []
     for side in range(2):
@@ -236,8 +264,10 @@
         copies.append(halo("c", corner, cs, cr, halo_sem, halo_in_sem))
         copies[-1].start()
     for side in range(2):
-        ys[side, 0:LEV, :] = strip(edge_tile, side)
-        ys[side, LEV:, :] = diffusivity[:, side * LANES : (side + 1) * LANES]
+        ys[side, 0:LEV, :] = strip(edge_tile, side).astype(BF16)
+        for k in range(2):
+            part_rows = rate_parts[k][:, side * LANES : (side + 1) * LANES]
+            ys[side, LEV + k * CX : LEV + (k + 1) * CX, :] = part_rows
         copies.append(halo("y", side, ys, yr, halo_sem, halo_in_sem))
         copies[-1].start()
 
@@ -252,24 +282,27 @@
     w_last[...] = dot(unit, w_last_t[...], (1, 1)).astype(BF16)
     for k in range(4):
         bias[k] = jnp.sum(jnp.where(same, b_inner[k : k + 1, :], 0.0), axis=1, keepdims=True)
-    same_lev = sublanes((LEV, LEV)) == lanes((LEV, LEV))
     bias[4, 0:LEV, :] = jnp.sum(jnp.where(same_lev, b_last[...], 0.0), axis=1, keepdims=True)
     total[...] = jnp.zeros_like(total)
 
     for copy in copies:
         copy.wait_recv()
-    rates[0:2, 0:CY] = xr[0, 2 * LEV + 6 :, :]
+    def arrived_rates(message, first):
+        high, rest = (message[first + k * CX : first + (k + 1) * CX, :].astype(F32) for k in range(2))
+        return high + rest
+
+    rates[0:2, 0:CY] = arrived_rates(xr.at[0], 2 * LEV)[CX - 2 :, :]
     rates[2 : CX + 2, 0:CY] = diffusivity[...]
-    rates[CX + 2 : CX + 4, 0:CY] = xr[1, 2 * LEV : 2 * LEV + 2, :]
+    rates[CX + 2 : CX + 4, 0:CY] = arrived_rates(xr.at[1], 2 * LEV)[0:2, :]
     first_rows = lanes((CX, LANES)) < LEV
     rates[0:8, CY:] = jnp.zeros((8, LANES), F32)
     rates[16:24, CY:] = jnp.zeros((8, LANES), F32)
-    rates[2 : CX + 2, CY:] = jnp.where(first_rows, yr[1, LEV:, :], yr[0, LEV:, :])
+    rates[2 : CX + 2, CY:] = jnp.where(
+        first_rows, arrived_rates(yr.at[1], LEV), arrived_rates(yr.at[0], LEV)
+    )
     one_row = lanes((1, LANES)) < LEV
-    rates[1:2, CY:] = jnp.where(one_row, cr[1, LEV + 7 :, :], cr[0, LEV + 7 :, :])
-    rates[CX + 2 : CX + 3, CY:] = jnp.where(
-        one_row, cr[3, LEV : LEV + 1, :], cr[2, LEV : LEV + 1, :]
-    )
+    rates[1:2, CY:] = jnp.where(one_row, cr[1, 1:2, :], cr[0, 1:2, :])
+    rates[CX + 2 : CX + 3, CY:] = jnp.where(one_row, cr[3, 1:2, :], cr[2, 1:2, :])
 
     def spread_halo(x_in, y_in, c_in):
         for side in range(2):
@@ -279,9 +312,11 @@
             outer = 0 if side == 0 else CX + 3
             field[outer, :, CY:] = jnp.zeros((LEV, LANES), F32)
             inner = 1 if side == 0 else CX + 2
-            field[inner, :, CY:] = jnp.where(
-                low, c_in[2 * side + 1, 0:LEV, :].astype(F32), c_in[2 * side, 0:LEV, :].astype(F32)
-            )
+            cell = [
+                jnp.sum(jnp.where(same_lev, c_in[2 * side + k, 0:1, 0:LEV], 0.0), axis=1, keepdims=True)
+                for k in range(2)
+            ]
+            field[inner, :, CY:] = jnp.where(low, cell[1], cell[0])
         from_left, from_right = y_in[0, 0:LEV, :].astype(F32), y_in[1, 0:LEV, :].astype(F32)
         for x in range(CX):
             field[x + 2, :, CY:] = halo_tile(from_left, from_right, x)
@@ -293,25 +328,28 @@
         near = ref[slab - 1] + ref[slab + 1] + near_sum(now)
         return now + rates[pl.ds(slab, 1), :] * (near - 4.0 * now)
 
-    def forward_first(slab, carry):
-        middle[slab] = diffused(field, slab)
-        return carry
-
-    lax.fori_loop(1, CX + 3, forward_first, 0)
-
-    def forward_second(x, carry):
-        later = diffused(middle, x + 2)[:, 0:CY]
-        both = jnp.concatenate([later, later - cells(targets, x)], axis=0)
-        columns[pl.ds(pl.multiple_of(x * CY, CY), CY), :] = both.T
-        return carry
-
-    lax.fori_loop(0, CX, forward_second, 0)
+    def forward_first(pair, carry):
+        done = [diffused(field, 2 * pair + k) for k in (1, 2)]
+        for k in (1, 2):
+            middle[2 * pair + k] = done[k - 1]
+        return carry
+
+    lax.fori_loop(0, CX // 2 + 1, forward_first, 0)
+
+    def forward_second(pair, carry):
+        for x in (2 * pair, 2 * pair + 1):
+            later = diffused(middle, x + 2)[:, 0:CY]
+            both = jnp.concatenate([later, later - cells(targets, x)], axis=0)
+            columns[pl.ds(pl.multiple_of(x * CY, CY), CY), :] = both.T
+        return carry
+
+    lax.fori_loop(0, CX // 2, forward_second, 0)
 
     def outgoing(j):
-        return remote(send.at[j], recv.at[j], out_sem.at[j], in_sem.at[j], (tile, wrapped(sub, j, SUBS)))
+        return remote(send.at[j], recv.at[j], out_sem.at[j], in_sem.at[j], (tile, partner(sub, j, 1)))
 
     def returning(j):
-        return remote(answer.at[j], back.at[j], ret_sem.at[j], back_sem.at[j], (tile, wrapped(sub, -j, SUBS)))
+        return remote(answer.at[j], back.at[j], ret_sem.at[j], back_sem.at[j], (tile, partner(sub, j, -1)))
 
     def gathered(table, line, source, target):
         for first in range(0, LANES, 16):
@@ -435,8 +473,29 @@
         for k in range(2):
             field[x + k + 2, :, 0:CY] = turned[k * LEV : (k + 1) * LEV]
 
-    copies = list(copies)
     ghalos = []
+
+    def home_row(line, k):
+        return rows[pl.ds(routes[1, line, k], 1), :]
+
+    for corner in range(4):
+        line = (0 if corner < 2 else 2 * CX - 2) + corner % 2
+        gcs[corner, 0:1, :] = home_row(line, (LANES - 1) * (corner % 2))
+        ghalos.append(halo("c", corner, gcs, gcr, ghalo_sem, ghalo_in_sem))
+        ghalos[-1].start()
+    edges[2 * 2 * CX :, :] = jnp.zeros((LANES - 4 * CX, LANES), F32)
+    for side in range(2):
+        taken = [
+            home_row(2 * x + side, (LANES - 2) * side + k) for x in range(CX) for k in range(2)
+        ]
+        for k in range(2 * CX):
+            edges[2 * CX * side + k : 2 * CX * side + k + 1, :] = taken[k]
+    turned_edges = edges[...].T[0:LEV, :]
+    for side in range(2):
+        moved = pltpu.roll(turned_edges, LANES - 2 * CX, 1) if side else turned_edges
+        gys[side] = moved.astype(BF16)
+        ghalos.append(halo("y", side, gys, gyr, ghalo_sem, ghalo_in_sem))
+        ghalos[-1].start()
 
     def home_edge(side, carry):
         home(side * (CX - 2))
@@ -447,13 +506,8 @@
         x = 0 if side == 0 else CX - 2
         for k in range(2):
             gxs[side, k * LEV : (k + 1) * LEV, :] = field[x + k + 2, :, 0:CY].astype(BF16)
-        for edge in range(2):
-            gcs[2 * side + edge] = edge_tile(0 if side == 0 else CX - 1, edge).astype(BF16)
         ghalos.append(halo("x", side, gxs, gxr, ghalo_sem, ghalo_in_sem))
-        for edge in range(2):
-            ghalos.append(halo("c", 2 * side + edge, gcs, gcr, ghalo_sem, ghalo_in_sem))
-        for copy in ghalos[-3:]:
-            copy.start()
+        ghalos[-1].start()
 
     mine = pl.multiple_of(tile * CHUNK, CHUNK)
     summed = wide[pl.ds(mine, CHUNK), :].astype(F32)
@@ -469,11 +523,6 @@
         return carry
 
     lax.fori_loop(1, CX // 2 - 1, home_pair, 0)
-    for side in range(2):
-        gys[side] = strip(edge_tile, side).astype(BF16)
-        ghalos.append(halo("y", side, gys, gyr, ghalo_sem, ghalo_in_sem))
-        ghalos[-1].start()
-
     for j in range(1, TILES):
         share_of(j).wait_recv()
     for j in range(TILES):
@@ -505,19 +554,23 @@
         near = rate[0] * ref[slab - 1] + rate[2] * ref[slab + 1] + near_sum(flow)
         return now + (near - 4.0 * flow)
 
-    def adjoint_first(slab, carry):
-        middle[slab] = adjoint(field, slab)
-        return carry
-
-    lax.fori_loop(1, CX + 3, adjoint_first, 0)
-
-    def adjoint_second(x, carry):
-        done = adjoint(middle, x + 2)
-        for h in range(2):
-            result[pl.ds(tiled_row(x, h), LEV, stride=2 * CX), :] = done[:, h * LANES : (h + 1) * LANES]
-        return carry
-
-    lax.fori_loop(0, CX, adjoint_second, 0)
+    def adjoint_first(pair, carry):
+        done = [adjoint(field, 2 * pair + k) for k in (1, 2)]
+        for k in (1, 2):
+            middle[2 * pair + k] = done[k - 1]
+        return carry
+
+    lax.fori_loop(0, CX // 2 + 1, adjoint_first, 0)
+
+    def adjoint_second(pair, carry):
+        done = [adjoint(middle, 2 * pair + k + 2) for k in range(2)]
+        for k in range(2):
+            for h in range(2):
+                row = tiled_row(2 * pair + k, h)
+                result[pl.ds(row, LEV, stride=2 * CX), :] = done[k][:, h * LANES : (h + 1) * LANES]
+        return carry
+
+    lax.fori_loop(0, CX // 2, adjoint_second, 0)
 
     stores[0].start()
 
@@ -596,12 +649,12 @@
             pltpu.VMEM((2, NCOL // LANES, LANES), jnp.int32),
             pltpu.SMEM((2, NCOL // LANES, LANES), jnp.int32),
         ]
-        + both_ways((2, 2 * LEV + 8, CY), F32)
-        + both_ways((2, LEV + CX, LANES), F32)
-        + both_ways((4, LEV + 8, LANES), F32)
+        + both_ways((2, 2 * LEV + 2 * CX, CY), BF16)
+        + both_ways((2, LEV + 2 * CX, LANES), BF16)
+        + both_ways((4, 8, LANES), F32)
         + both_ways((2, 2 * LEV, CY), BF16)
         + both_ways((2, LEV, LANES), BF16)
-        + both_ways((4, LEV, LANES), BF16)
+        + both_ways((4, 8, LANES), F32)
         + [
             pltpu.VMEM((WIDTH, LEV), BF16),
             pltpu.VMEM((3, WIDTH, WIDTH), BF16),
@@ -614,6 +667,7 @@
         + [
             pltpu.VMEM((NCOL, LANES), F32),
             pltpu.VMEM((4, LANES, LANES), F32),
+            pltpu.VMEM((LANES, LANES), F32),
             pltpu.VMEM((GRAD_ROWS, 256), F32),
             pltpu.VMEM((GRAD_ROWS, 256), BF16),
         ]

time: 70.7 us -> 63 us (0.89); the launches traced: 69.6 us -> 62.8 us
  Pallas kernels: 69 us -> 62.2 us
    pallas_call x1, Pallas kernels: 66.5 us -> 59.6 us  [per_device(): pl.pallas_call(step_kernel, out_shape=(jax.ShapeDtypeStruct((LEV * CX * 2...]
where the time goes in v2:
time: 63 us; the launch traced here: 62.8 us
  Pallas kernels  62.2 us (99%)
  between operations  0.64 us (1%)
    pallas_call x1, Pallas kernels, per_device(): pl.pallas_call(step_kernel, out_shape=(jax.ShapeDtypeStruct((LEV * CX * 2...  59.6 us
    pallas_call x1, Pallas kernels, per_device(): pl.pallas_call(copy_kernel, out_shape=tuple((jax.ShapeDtypeStruct(one.sha...  2.52 us

profile of v2, /device:TPU:0, one launch (start us, length us, event | category | flops | bytes accessed | tf_op | source)
XLA Modules:
  0.0 62.8 jit_solution(5449104459494259262)
XLA Ops:
  0.6 59.6 %step.1 = (f32[2048,128]{1,0:T(8,128)}, f32[64,192]{1,0:T(8,128)}, f32[3,192,192]{2,1,0:T(8,128)}, f32[64,192]{1,0:T(8,128)}, f32[4,192]{1,0:T(4,128)}, /*index=5*/f32[1,64]{1,0:T(1,128)}) custom-call(f32[2048,128]{1,0:T(8,128)} %bitcast.27, f32[2048,128]{1,0:T(8,128)} %bitcast.28, f32[16,256]{1,0:T(8,128)} %diffusivity_hbm.1, s32[1,4096]{1,0:T(1,128)} %order_hbm.1, ...), custom_call_target="tpu_custom_call" | custom-call | tf_op jit(solution)/shard_map/step/pallas_call | solution.py:614
  60.3 2.5 %finish.1 = (f32[2048,128]{1,0:T(8,128)}, f32[64,192]{1,0:T(8,128)}, f32[3,192,192]{2,1,0:T(8,128)}, f32[64,192]{1,0:T(8,128)}, f32[4,192]{1,0:T(4,128)}, /*index=5*/f32[1,64]{1,0:T(1,128)}) custom-call(f32[2048,128]{1,0:T(8,128)} %get-tuple-element.18.refs_0_, f32[64,192]{1,0:T(8,128)} %get-tuple-element.19.refs_1_, ...), custom_call_target="tpu_custom_call" | custom-call | tf_op jit(solution)/shard_map/finish/pallas_call | solution.py:695

commit v3 on v2

--- a/solution.py
+++ b/solution.py
@@ -45,22 +45,30 @@
     )
 
 
-def gray(step):
-    return step + step // 2 - 2 * (step // 3)
-
-
-def partner(sub, j, sign):
+PAIRS = ((0, 0), (2, 0), (2, 1), (1, 0), (3, 0), (1, 1), (3, 1), (0, 1))
+
+
+def crossing(j):
     late = jnp.minimum(j // 2, 1)
-    turned = late * (1 - j % 2) + (1 - late) * (j % 2)
-    x = gray(j // 2 % 4)
+    return late * (1 - j % 2) + (1 - late) * (j % 2)
+
+
+def partner(tile, sub, j, sign):
+    turned = crossing(j)
+    x = sum(jnp.where(j // 2 == k, pair[0], 0) for k, pair in enumerate(PAIRS))
+    core = sum(jnp.where(j // 2 == k, pair[1], 0) for k, pair in enumerate(PAIRS))
     high = (sub // 8 + turned) % 2
     middle = (sub // 2 + sign * x + 4) % 4
-    return high * 8 + middle * 2 + (sub + j // 8) % 2
+    return (tile + 4 * turned) % TILES, high * 8 + middle * 2 + (sub + core) % 2
 
 
 def place_of(sub, other):
     turned = (other // 8 + sub // 8) % 2
-    step = (other + sub) % 2 * 4 + gray((other // 2 - sub // 2 + 8) % 4)
+    x = (other // 2 - sub // 2 + 8) % 4
+    core = (other + sub) % 2
+    step = sum(
+        jnp.where((x == pair[0]) & (core == pair[1]), k, 0) for k, pair in enumerate(PAIRS)
+    )
     late = jnp.minimum(step, 1)
     return 2 * step + late * (1 - turned) + (1 - late) * turned
 
@@ -155,7 +163,7 @@
     field, middle, rates, columns, tables, routes,
     xs, xr, ys, yr, cs, cr, gxs, gxr, gys, gyr, gcs, gcr,
     wt_first, wt_inner, w_last, bias,
-    stage, send, recv, answer, back, rows, grads, edges, total, wide, parts, whole,
+    stage, send, recv, answer, back, rows, grads_even, grads_odd, edges, total, wide, parts, whole,
     table_sem, halo_sem, halo_in_sem, ghalo_sem, ghalo_in_sem,
     out_sem, in_sem, ret_sem, back_sem, part_sem, part_in_sem, whole_sem, whole_in_sem,
 ):
@@ -167,9 +175,9 @@
         (down, left), (down, right), (up, left), (up, right),
     )
     peers = (
-        [(tile, wrapped(sub, j, SUBS)) for j in range(1, SUBS)]
+        [partner(tile, sub, j, 1) for j in range(1, SUBS)]
         + [(wrapped(tile, j, TILES), sub) for j in range(1, TILES)]
-        + list(around[4:])
+        + list(around[2:])
     )
     barrier = pltpu.get_barrier_semaphore()
     for peer in peers:
@@ -274,17 +282,6 @@
     for load in loads[2:]:
         load.wait()
     find_routes(order, counts, sub, routes, tables, table_sem)
-    same = sublanes((WIDTH, WIDTH)) == lanes((WIDTH, WIDTH))
-    unit = same.astype(F32).astype(BF16)
-    wt_first[...] = dot(unit, w_first[...], (1, 1)).astype(BF16)
-    for k in range(3):
-        wt_inner[k] = dot(unit, w_inner[k], (1, 1)).astype(BF16)
-    w_last[...] = dot(unit, w_last_t[...], (1, 1)).astype(BF16)
-    for k in range(4):
-        bias[k] = jnp.sum(jnp.where(same, b_inner[k : k + 1, :], 0.0), axis=1, keepdims=True)
-    bias[4, 0:LEV, :] = jnp.sum(jnp.where(same_lev, b_last[...], 0.0), axis=1, keepdims=True)
-    total[...] = jnp.zeros_like(total)
-
     for copy in copies:
         copy.wait_recv()
     def arrived_rates(message, first):
@@ -346,10 +343,10 @@
     lax.fori_loop(0, CX // 2, forward_second, 0)
 
     def outgoing(j):
-        return remote(send.at[j], recv.at[j], out_sem.at[j], in_sem.at[j], (tile, partner(sub, j, 1)))
+        return remote(send.at[j], recv.at[j], out_sem.at[j], in_sem.at[j], partner(tile, sub, j, 1))
 
     def returning(j):
-        return remote(answer.at[j], back.at[j], ret_sem.at[j], back_sem.at[j], (tile, partner(sub, j, -1)))
+        return remote(answer.at[j], back.at[j], ret_sem.at[j], back_sem.at[j], partner(tile, sub, j, -1))
 
     def gathered(table, line, source, target):
         for first in range(0, LANES, 16):
@@ -371,6 +368,17 @@
 
     lax.fori_loop(1, SUBS + 1, push, 0)
     recv[0] = send[0]
+
+    same = sublanes((WIDTH, WIDTH)) == lanes((WIDTH, WIDTH))
+    unit = same.astype(F32).astype(BF16)
+    wt_first[...] = dot(unit, w_first[...], (1, 1)).astype(BF16)
+    for k in range(3):
+        wt_inner[k] = dot(unit, w_inner[k], (1, 1)).astype(BF16)
+    w_last[...] = dot(unit, w_last_t[...], (1, 1)).astype(BF16)
+    for k in range(4):
+        bias[k] = jnp.sum(jnp.where(same, b_inner[k : k + 1, :], 0.0), axis=1, keepdims=True)
+    bias[4, 0:LEV, :] = jnp.sum(jnp.where(same_lev, b_last[...], 0.0), axis=1, keepdims=True)
+    total[...] = jnp.zeros_like(total)
 
     extra = (sublanes((AUG, SHARE)) == 0).astype(F32).astype(BF16)
 
@@ -461,17 +469,17 @@
     lax.fori_loop(1, SUBS, take, 0)
 
     left_half = lanes((CY, LANES)) < LEV
-
-    def home(x):
-        def some(line, carry):
-            gathered(1, x * 2 + line, rows, grads.at[line])
-            return carry
-
-        lax.fori_loop(0, 4, some, 0)
-        slab = [grads[2 * k : 2 * k + 2].reshape(CY, LANES) for k in range(2)]
-        turned = jnp.where(left_half, slab[0], pltpu.roll(slab[1], LEV, 1)).T
-        for k in range(2):
-            field[x + k + 2, :, 0:CY] = turned[k * LEV : (k + 1) * LEV]
+    grads = (grads_even, grads_odd)
+
+    def home(first_slabs):
+        for held, x in zip(grads, first_slabs):
+            for line in range(4):
+                gathered(1, x * 2 + line, rows, held.at[line])
+        for held, x in zip(grads, first_slabs):
+            slab = [held[2 * k : 2 * k + 2].reshape(CY, LANES) for k in range(2)]
+            turned = jnp.where(left_half, slab[0], pltpu.roll(slab[1], LEV, 1)).T
+            for k in range(2):
+                field[x + k + 2, :, 0:CY] = turned[k * LEV : (k + 1) * LEV]
 
     ghalos = []
 
@@ -497,11 +505,7 @@
         ghalos.append(halo("y", side, gys, gyr, ghalo_sem, ghalo_in_sem))
         ghalos[-1].start()
 
-    def home_edge(side, carry):
-        home(side * (CX - 2))
-        return carry
-
-    lax.fori_loop(0, 2, home_edge, 0)
+    home((0, CX - 2))
     for side in range(2):
         x = 0 if side == 0 else CX - 2
         for k in range(2):
@@ -518,11 +522,30 @@
     for j in range(1, TILES):
         share_of(j).start()
 
-    def home_pair(pair, carry):
-        home(2 * pair)
-        return carry
-
-    lax.fori_loop(1, CX // 2 - 1, home_pair, 0)
+    def home_pairs(turn, carry):
+        home((4 * turn + 2, 4 * turn + 4))
+        return carry
+
+    lax.fori_loop(0, CX // 4 - 1, home_pairs, 0)
+    for copy in ghalos:
+        copy.wait_recv()
+    spread_halo(gxr, gyr, gcr)
+
+    def adjoint(ref, slab):
+        rate = [rates[pl.ds(slab + k, 1), :] for k in (-1, 0, 1)]
+        now = ref[slab]
+        flow = rate[1] * now
+        near = rate[0] * ref[slab - 1] + rate[2] * ref[slab + 1] + near_sum(flow)
+        return now + (near - 4.0 * flow)
+
+    def adjoint_first(pair, carry):
+        done = [adjoint(field, 2 * pair + k) for k in (1, 2)]
+        for k in (1, 2):
+            middle[2 * pair + k] = done[k - 1]
+        return carry
+
+    lax.fori_loop(0, CX // 2 + 1, adjoint_first, 0)
+
     for j in range(1, TILES):
         share_of(j).wait_recv()
     for j in range(TILES):
@@ -542,25 +565,6 @@
     step_bias_last[...] = jnp.sum(jnp.where(same_lev, last_bias, 0.0), axis=0, keepdims=True)
     for store in stores[1:]:
         store.start()
-
-    for copy in ghalos:
-        copy.wait_recv()
-    spread_halo(gxr, gyr, gcr)
-
-    def adjoint(ref, slab):
-        rate = [rates[pl.ds(slab + k, 1), :] for k in (-1, 0, 1)]
-        now = ref[slab]
-        flow = rate[1] * now
-        near = rate[0] * ref[slab - 1] + rate[2] * ref[slab + 1] + near_sum(flow)
-        return now + (near - 4.0 * flow)
-
-    def adjoint_first(pair, carry):
-        done = [adjoint(field, 2 * pair + k) for k in (1, 2)]
-        for k in (1, 2):
-            middle[2 * pair + k] = done[k - 1]
-        return carry
-
-    lax.fori_loop(0, CX // 2 + 1, adjoint_first, 0)
 
     def adjoint_second(pair, carry):
         done = [adjoint(middle, 2 * pair + k + 2) for k in range(2)]
@@ -667,6 +671,7 @@
         + [
             pltpu.VMEM((NCOL, LANES), F32),
             pltpu.VMEM((4, LANES, LANES), F32),
+            pltpu.VMEM((4, LANES, LANES), F32),
             pltpu.VMEM((LANES, LANES), F32),
             pltpu.VMEM((GRAD_ROWS, 256), F32),
             pltpu.VMEM((GRAD_ROWS, 256), BF16),

time: 63 us -> 59.4 us (0.943); the launches traced: 62.8 us -> 58.3 us
  Pallas kernels: 62.2 us -> 57.6 us
    pallas_call x1, Pallas kernels: 59.6 us -> 55.1 us  [per_device(): pl.pallas_call(step_kernel, out_shape=(jax.ShapeDtypeStruct((LEV * CX * 2...]
where the time goes in v3:
time: 59.4 us; the launch traced here: 58.3 us
  Pallas kernels  57.6 us (97%)
  between operations  0.64 us (1%)
    pallas_call x1, Pallas kernels, per_device(): pl.pallas_call(step_kernel, out_shape=(jax.ShapeDtypeStruct((LEV * CX * 2...  55.1 us
    pallas_call x1, Pallas kernels, per_device(): pl.pallas_call(copy_kernel, out_shape=tuple((jax.ShapeDtypeStruct(one.sha...  2.52 us

profile of v3, /device:TPU:0, one launch (start us, length us, event | category | flops | bytes accessed | tf_op | source)
XLA Modules:
  0.0 58.3 jit_solution(6187168187418350777)
XLA Ops:
  0.6 55.1 %step.1 = (f32[2048,128]{1,0:T(8,128)}, f32[64,192]{1,0:T(8,128)}, f32[3,192,192]{2,1,0:T(8,128)}, f32[64,192]{1,0:T(8,128)}, f32[4,192]{1,0:T(4,128)}, /*index=5*/f32[1,64]{1,0:T(1,128)}) custom-call(f32[2048,128]{1,0:T(8,128)} %bitcast.27, f32[2048,128]{1,0:T(8,128)} %bitcast.28, f32[16,256]{1,0:T(8,128)} %diffusivity_hbm.1, s32[1,4096]{1,0:T(1,128)} %order_hbm.1, ...), custom_call_target="tpu_custom_call" | custom-call | tf_op jit(solution)/shard_map/step/pallas_call | solution.py:618
  55.8 2.5 %finish.1 = (f32[2048,128]{1,0:T(8,128)}, f32[64,192]{1,0:T(8,128)}, f32[3,192,192]{2,1,0:T(8,128)}, f32[64,192]{1,0:T(8,128)}, f32[4,192]{1,0:T(4,128)}, /*index=5*/f32[1,64]{1,0:T(1,128)}) custom-call(f32[2048,128]{1,0:T(8,128)} %get-tuple-element.18.refs_0_, f32[64,192]{1,0:T(8,128)} %get-tuple-element.19.refs_1_, ...), custom_call_target="tpu_custom_call" | custom-call | tf_op jit(solution)/shard_map/finish/pallas_call | solution.py:700

commit v4 on v3

--- a/solution.py
+++ b/solution.py
@@ -21,9 +21,12 @@
 LANES = 128
 SPAN = CY + LANES
 SLABS = CX + 4
-CHUNK = 96
+CHUNK = 144
+GRAD_ROWS = 768
+UPPER = GRAD_ROWS // 2
+PACKED_ROWS = CHUNK * TILES
+LAST_BIAS = LEV + 2
 GROUP = 4
-GRAD_ROWS = CHUNK * TILES
 FIRST_INNER = LEV + AUG
 FIRST_LAST = FIRST_INNER + 3 * (WIDTH + AUG)
 ANY = pl.BlockSpec(memory_space=pl.ANY)
@@ -163,7 +166,7 @@
     field, middle, rates, columns, tables, routes,
     xs, xr, ys, yr, cs, cr, gxs, gxr, gys, gyr, gcs, gcr,
     wt_first, wt_inner, w_last, bias,
-    stage, send, recv, answer, back, rows, grads_even, grads_odd, edges, total, wide, parts, whole,
+    stage, send, recv, answer, back, rows, grads_even, grads_odd, edges, total, wide, flat, parts, whole,
     table_sem, halo_sem, halo_in_sem, ghalo_sem, ghalo_in_sem,
     out_sem, in_sem, ret_sem, back_sem, part_sem, part_in_sem, whole_sem, whole_in_sem,
 ):
@@ -179,10 +182,6 @@
         + [(wrapped(tile, j, TILES), sub) for j in range(1, TILES)]
         + list(around[2:])
     )
-    barrier = pltpu.get_barrier_semaphore()
-    for peer in peers:
-        pl.semaphore_signal(barrier, inc=1, device_id=peer, device_id_type=MESH)
-
     loads = [
         pltpu.make_async_copy(source, target, load_sem.at[k])
         for k, (source, target) in enumerate(
@@ -196,6 +195,9 @@
     ]
     for load in loads:
         load.start()
+    barrier = pltpu.get_barrier_semaphore()
+    for peer in peers:
+        pl.semaphore_signal(barrier, inc=1, device_id=peer, device_id_type=MESH)
     stores = [
         pltpu.make_async_copy(source, target, store_sem.at[k])
         for k, (source, target) in enumerate(
@@ -246,7 +248,8 @@
 
     loads[0].wait()
     loads[1].wait()
-    lax.fori_loop(0, CX, fill, 0)
+    for x in (0, 1, CX - 2, CX - 1):
+        fill(x, 0)
     rate_high = diffusivity[...].astype(BF16)
     rate_parts = (rate_high, (diffusivity[...] - rate_high.astype(F32)).astype(BF16))
     same_lev = sublanes((LEV, LEV)) == lanes((LEV, LEV))
@@ -271,6 +274,7 @@
     for corner in range(4):
         copies.append(halo("c", corner, cs, cr, halo_sem, halo_in_sem))
         copies[-1].start()
+    lax.fori_loop(2, CX - 2, fill, 0)
     for side in range(2):
         ys[side, 0:LEV, :] = strip(edge_tile, side).astype(BF16)
         for k in range(2):
@@ -436,7 +440,13 @@
 
     lax.fori_loop(0, SUBS // GROUP, some_blocks, 0)
 
-    wide[...] = total[...].astype(BF16)
+    last_bias = jnp.where(same_lev, total[FIRST_LAST:, WIDTH : WIDTH + 1], 0.0)
+    total[LAST_BIAS : LAST_BIAS + 1, 0:LEV] = jnp.sum(last_bias, axis=0, keepdims=True)
+    upper_low = lanes((UPPER, LANES)) < LEV
+    wide[0:GRAD_ROWS, :] = total[:, 0:LANES].astype(BF16)
+    wide[GRAD_ROWS:, :] = jnp.where(
+        upper_low, total[0:UPPER, LANES:], pltpu.roll(total[UPPER:, LANES:], LEV, 1)
+    ).astype(BF16)
 
     def part(j):
         owner = wrapped(tile, j, TILES)
@@ -550,8 +560,11 @@
         share_of(j).wait_recv()
     for j in range(TILES):
         owner = wrapped(tile, -j, TILES)
-        total[pl.ds(pl.multiple_of(owner * CHUNK, CHUNK), CHUNK), :] = whole[j].astype(F32)
-    everything = total[...]
+        flat[pl.ds(pl.multiple_of(owner * CHUNK, CHUNK), CHUNK), :] = whole[j].astype(F32)
+    everything = flat[...]
+    total[:, 0:LANES] = flat[0:GRAD_ROWS, :]
+    total[0:UPPER, LANES:] = flat[GRAD_ROWS:, :]
+    total[UPPER:, LANES:] = pltpu.roll(flat[GRAD_ROWS:, :], LEV, 1)
     squares = jnp.sum(jnp.sum(everything * everything, axis=0, keepdims=True), axis=1, keepdims=True)
     factor = lax.rsqrt(squares / PARAMS + 1e-06)
     step_first[...] = total[0:LEV, 0:WIDTH] * factor
@@ -561,8 +574,7 @@
         step_inner[k] = total[row : row + WIDTH, 0:WIDTH] * factor
         step_bias_inner[k + 1 : k + 2, :] = total[row + WIDTH : row + WIDTH + 1, 0:WIDTH] * factor
     step_last_t[...] = total[FIRST_LAST:, 0:WIDTH] * factor
-    last_bias = total[FIRST_LAST:, WIDTH : WIDTH + 1] * factor
-    step_bias_last[...] = jnp.sum(jnp.where(same_lev, last_bias, 0.0), axis=0, keepdims=True)
+    step_bias_last[...] = total[LAST_BIAS : LAST_BIAS + 1, 0:LEV] * factor
     for store in stores[1:]:
         store.start()
 
@@ -596,8 +608,13 @@
 def copy_kernel(*refs):
     sources, targets, held = refs[0:6], refs[6:12], refs[12:18]
     in_sem, out_sem = refs[18:]
-    loads = [pltpu.make_async_copy(sources[k], held[k], in_sem.at[k]) for k in range(6)]
-    stores = [pltpu.make_async_copy(held[k], targets[k], out_sem.at[k]) for k in range(6)]
+    piece = LEV * CX * 2 // 4
+    places = [(0, pl.ds(k * piece, piece)) for k in range(4)] + [(k, slice(None)) for k in range(1, 6)]
+    loads, stores = [], []
+    for k, (which, rows) in enumerate(places):
+        source, middle, target = (group[which].at[rows] for group in (sources, held, targets))
+        loads.append(pltpu.make_async_copy(source, middle, in_sem.at[k]))
+        stores.append(pltpu.make_async_copy(middle, target, out_sem.at[k]))
     for load in loads:
         load.start()
     for load, store in zip(loads, stores):
@@ -674,9 +691,10 @@
             pltpu.VMEM((4, LANES, LANES), F32),
             pltpu.VMEM((LANES, LANES), F32),
             pltpu.VMEM((GRAD_ROWS, 256), F32),
-            pltpu.VMEM((GRAD_ROWS, 256), BF16),
+            pltpu.VMEM((PACKED_ROWS, LANES), BF16),
+            pltpu.VMEM((PACKED_ROWS, LANES), F32),
         ]
-        + both_ways((TILES, CHUNK, 256), BF16)
+        + both_ways((TILES, CHUNK, LANES), BF16)
         + [pltpu.SemaphoreType.DMA((2,))]
         + [pltpu.SemaphoreType.DMA((8,))] * 4
         + [pltpu.SemaphoreType.DMA((SUBS,))] * 4
@@ -703,7 +721,7 @@
         in_specs=[ANY] * 6,
         out_specs=(ANY,) * 6,
         scratch_shapes=[pltpu.VMEM(one.shape, one.dtype) for one in made]
-        + [pltpu.SemaphoreType.DMA((6,))] * 2,
+        + [pltpu.SemaphoreType.DMA((9,))] * 2,
         name="finish",
     )(*made)
     return (

time: 59.4 us -> 58.1 us (0.978); the launches traced: 58.3 us -> 57.7 us
  no operation moved by 1% of the time
where the time goes in v4:
time: 58.1 us; the launch traced here: 57.7 us
  Pallas kernels  57.1 us (98%)
  between operations  0.64 us (1%)
    pallas_call x1, Pallas kernels, per_device(): pl.pallas_call(step_kernel, out_shape=(jax.ShapeDtypeStruct((LEV * CX * 2...  54.7 us
    pallas_call x1, Pallas kernels, per_device(): pl.pallas_call(copy_kernel, out_shape=tuple((jax.ShapeDtypeStruct(one.sha...  2.39 us

profile of v4, /device:TPU:0, one launch (start us, length us, event | category | flops | bytes accessed | tf_op | source)
XLA Modules:
  0.0 57.7 jit_solution(13962924172869353123)
XLA Ops:
  0.6 54.7 %step.1 = (f32[2048,128]{1,0:T(8,128)}, f32[64,192]{1,0:T(8,128)}, f32[3,192,192]{2,1,0:T(8,128)}, f32[64,192]{1,0:T(8,128)}, f32[4,192]{1,0:T(4,128)}, /*index=5*/f32[1,64]{1,0:T(1,128)}) custom-call(f32[2048,128]{1,0:T(8,128)} %bitcast.27, f32[2048,128]{1,0:T(8,128)} %bitcast.28, f32[16,256]{1,0:T(8,128)} %diffusivity_hbm.1, s32[1,4096]{1,0:T(1,128)} %order_hbm.1, ...), custom_call_target="tpu_custom_call" | custom-call | tf_op jit(solution)/shard_map/step/pallas_call | solution.py:635
  55.3 2.4 %finish.1 = (f32[2048,128]{1,0:T(8,128)}, f32[64,192]{1,0:T(8,128)}, f32[3,192,192]{2,1,0:T(8,128)}, f32[64,192]{1,0:T(8,128)}, f32[4,192]{1,0:T(4,128)}, /*index=5*/f32[1,64]{1,0:T(1,128)}) custom-call(f32[2048,128]{1,0:T(8,128)} %get-tuple-element.18.refs_0_, f32[64,192]{1,0:T(8,128)} %get-tuple-element.19.refs_1_, ...), custom_call_target="tpu_custom_call" | custom-call | tf_op jit(solution)/shard_map/finish/pallas_call | solution.py:718

commit v5 on v4

--- a/solution.py
+++ b/solution.py
@@ -556,6 +556,17 @@
 
     lax.fori_loop(0, CX // 2 + 1, adjoint_first, 0)
 
+    def adjoint_second(pair, carry):
+        done = [adjoint(middle, 2 * pair + k + 2) for k in range(2)]
+        for k in range(2):
+            for h in range(2):
+                row = tiled_row(2 * pair + k, h)
+                result[pl.ds(row, LEV, stride=2 * CX), :] = done[k][:, h * LANES : (h + 1) * LANES]
+        return carry
+
+    lax.fori_loop(0, CX // 2, adjoint_second, 0)
+
+    stores[0].start()
     for j in range(1, TILES):
         share_of(j).wait_recv()
     for j in range(TILES):
@@ -578,17 +589,6 @@
     for store in stores[1:]:
         store.start()
 
-    def adjoint_second(pair, carry):
-        done = [adjoint(middle, 2 * pair + k + 2) for k in range(2)]
-        for k in range(2):
-            for h in range(2):
-                row = tiled_row(2 * pair + k, h)
-                result[pl.ds(row, LEV, stride=2 * CX), :] = done[k][:, h * LANES : (h + 1) * LANES]
-        return carry
-
-    lax.fori_loop(0, CX // 2, adjoint_second, 0)
-
-    stores[0].start()
 
     def settle(j, carry):
         outgoing(j).wait_send()

time: 58.1 us -> 57.8 us (level)
  no operation moved by 1% of the time
where the time goes in v5:
time: 57.8 us; the launch traced here: 57.6 us
  Pallas kernels  57 us (99%)
  between operations  0.64 us (1%)
    pallas_call x1, Pallas kernels, per_device(): pl.pallas_call(step_kernel, out_shape=(jax.ShapeDtypeStruct((LEV * CX * 2...  54.6 us
    pallas_call x1, Pallas kernels, per_device(): pl.pallas_call(copy_kernel, out_shape=tuple((jax.ShapeDtypeStruct(one.sha...  2.39 us

profile of v5, /device:TPU:0, one launch (start us, length us, event | category | flops | bytes accessed | tf_op | source)
XLA Modules:
  0.0 57.6 jit_solution(12946922725134881842)
XLA Ops:
  0.6 54.6 %step.1 = (f32[2048,128]{1,0:T(8,128)}, f32[64,192]{1,0:T(8,128)}, f32[3,192,192]{2,1,0:T(8,128)}, f32[64,192]{1,0:T(8,128)}, f32[4,192]{1,0:T(4,128)}, /*index=5*/f32[1,64]{1,0:T(1,128)}) custom-call(f32[2048,128]{1,0:T(8,128)} %bitcast.27, f32[2048,128]{1,0:T(8,128)} %bitcast.28, f32[16,256]{1,0:T(8,128)} %diffusivity_hbm.1, s32[1,4096]{1,0:T(1,128)} %order_hbm.1, ...), custom_call_target="tpu_custom_call" | custom-call | tf_op jit(solution)/shard_map/step/pallas_call | solution.py:635
  55.2 2.4 %finish.1 = (f32[2048,128]{1,0:T(8,128)}, f32[64,192]{1,0:T(8,128)}, f32[3,192,192]{2,1,0:T(8,128)}, f32[64,192]{1,0:T(8,128)}, f32[4,192]{1,0:T(4,128)}, /*index=5*/f32[1,64]{1,0:T(1,128)}) custom-call(f32[2048,128]{1,0:T(8,128)} %get-tuple-element.18.refs_0_, f32[64,192]{1,0:T(8,128)} %get-tuple-element.19.refs_1_, ...), custom_call_target="tpu_custom_call" | custom-call | tf_op jit(solution)/shard_map/finish/pallas_call | solution.py:718

commit v6 on v5

--- a/solution.py
+++ b/solution.py
@@ -48,7 +48,7 @@
     )
 
 
-PAIRS = ((0, 0), (2, 0), (2, 1), (1, 0), (3, 0), (1, 1), (3, 1), (0, 1))
+PAIRS = ((0, 0), (2, 0), (1, 0), (3, 0), (2, 1), (1, 1), (3, 1), (0, 1))
 
 
 def crossing(j):

time: 57.8 us -> 57.2 us (0.990); the launches traced: 57.6 us -> 56.3 us
  Pallas kernels: 57 us -> 55.6 us
    pallas_call x1, Pallas kernels: 54.6 us -> 53.2 us  [per_device(): pl.pallas_call(step_kernel, out_shape=(jax.ShapeDtypeStruct((LEV * CX * 2...]
where the time goes in v6:
time: 57.2 us; the launch traced here: 56.3 us
  Pallas kernels  55.6 us (97%)
  between operations  0.64 us (1%)
    pallas_call x1, Pallas kernels, per_device(): pl.pallas_call(step_kernel, out_shape=(jax.ShapeDtypeStruct((LEV * CX * 2...  53.2 us
    pallas_call x1, Pallas kernels, per_device(): pl.pallas_call(copy_kernel, out_shape=tuple((jax.ShapeDtypeStruct(one.sha...  2.39 us

profile of v6, /device:TPU:0, one launch (start us, length us, event | category | flops | bytes accessed | tf_op | source)
XLA Modules:
  0.0 56.3 jit_solution(12654706845289729593)
XLA Ops:
  0.6 53.2 %step.1 = (f32[2048,128]{1,0:T(8,128)}, f32[64,192]{1,0:T(8,128)}, f32[3,192,192]{2,1,0:T(8,128)}, f32[64,192]{1,0:T(8,128)}, f32[4,192]{1,0:T(4,128)}, /*index=5*/f32[1,64]{1,0:T(1,128)}) custom-call(f32[2048,128]{1,0:T(8,128)} %bitcast.27, f32[2048,128]{1,0:T(8,128)} %bitcast.28, f32[16,256]{1,0:T(8,128)} %diffusivity_hbm.1, s32[1,4096]{1,0:T(1,128)} %order_hbm.1, ...), custom_call_target="tpu_custom_call" | custom-call | tf_op jit(solution)/shard_map/step/pallas_call | solution.py:635
  53.9 2.4 %finish.1 = (f32[2048,128]{1,0:T(8,128)}, f32[64,192]{1,0:T(8,128)}, f32[3,192,192]{2,1,0:T(8,128)}, f32[64,192]{1,0:T(8,128)}, f32[4,192]{1,0:T(4,128)}, /*index=5*/f32[1,64]{1,0:T(1,128)}) custom-call(f32[2048,128]{1,0:T(8,128)} %get-tuple-element.18.refs_0_, f32[64,192]{1,0:T(8,128)} %get-tuple-element.19.refs_1_, ...), custom_call_target="tpu_custom_call" | custom-call | tf_op jit(solution)/shard_map/finish/pallas_call | solution.py:718
